TPU v7x, 128 devices: a whole 4x4x4 slice. The times are simulated.
128 devices in a mesh: loop: 64 (over z_hi, x, y, core), group: 2 (over z_lo).
Axes of the slice: x: 4, y: 4, z: 4 (z_hi: 2, z_lo: 2; z = z_hi * 2 + z_lo), core: 2. Of those that a mesh axis runs over, the one named last changes fastest.
Arguments:
- references: bfloat16 [262144, 512], P(('loop', 'group')), may hold values from -40 to 40
- bank: bfloat16 [6144, 512], P('loop'), may hold values from -64 to 64
- queries: bfloat16 [1536, 512], P('loop'), may hold values from -64 to 64
Outputs:
- expanded: float32 [1536, 512], P(('loop', 'group'))
All inputs are finite; a program needn't handle non-finite values.
Results may differ from a plain program's by a relative error of at most 0.0019.
Values may be sent and summed in bfloat16 or wider, within the bound.
A program may use at most 64 MiB of HBM per device.

v0:
```python
import math

import jax
import jax.numpy as jnp
from jax import lax
from jax.sharding import PartitionSpec as P


def similar(rows, columns):
    return lax.dot_general(
        rows, columns, (((1,), (1,)), ((), ())), preferred_element_type=jnp.float32
    )


def block_size(count):
    return math.gcd(count, 512)


def per_device(references, bank, queries):
    ref_count, width = references.shape
    start_state = (
        jnp.full((ref_count,), -jnp.inf, jnp.float32),
        jnp.zeros((ref_count,), jnp.float32),
    )
    piece = lax.all_gather(bank, "loop", axis=0, tiled=True)
    piece_rows = piece.shape[0]
    row_step = block_size(piece_rows)
    row_blocks = piece.reshape(piece_rows // row_step, row_step, width)

    def add_absorb(carry, block):
        peak, total = carry
        scores = similar(block, references)
        new_peak = jnp.maximum(peak, jnp.max(scores, axis=0))
        total = total * jnp.exp(peak - new_peak) + jnp.sum(jnp.exp(scores - new_peak), axis=0)
        return ((new_peak, total), None)

    result, unused = lax.scan(add_absorb, start_state, row_blocks)
    peak, total = result
    offset = peak + jnp.log(total)
    all_queries = lax.all_gather(queries, "loop", axis=0, tiled=True)
    loop_size = lax.axis_size("loop")
    group_size = lax.axis_size("group")
    own_rows = all_queries.shape[0] // (loop_size * group_size)
    ref_step = block_size(ref_count)
    ref_blocks = references.reshape(ref_count // ref_step, ref_step, width)
    offset_blocks = offset.reshape(ref_count // ref_step, ref_step)

    def weighted_absorb(pooled, pair):
        block, shift = pair
        weights = jax.nn.sigmoid(similar(all_queries, block) - shift).astype(jnp.bfloat16)
        return (pooled + jnp.dot(weights, block, preferred_element_type=jnp.float32), None)

    pooled, unused = lax.scan(
        weighted_absorb,
        jnp.zeros((lax.axis_size(("loop", "group")) * own_rows, width), jnp.float32),
        (ref_blocks, offset_blocks),
    )
    pooled = lax.psum_scatter(pooled, ("loop", "group"), scatter_dimension=0, tiled=True)
    own_queries = lax.dynamic_slice_in_dim(queries, lax.axis_index("group") * own_rows, own_rows, 0)
    scale = lax.rsqrt(jnp.mean(pooled * pooled, axis=1, keepdims=True) + 1e-06)
    return own_queries.astype(jnp.float32) + pooled * scale


def solution(mesh):
    return jax.shard_map(
        per_device,
        mesh=mesh,
        in_specs=(P(("loop", "group"), None), P("loop", None), P("loop", None)),
        out_specs=P(("loop", "group"), None),
        check_vma=False,
    )
```

profile of v0, /device:TPU:1, one launch (start us, length us, event | category | flops | bytes accessed | tf_op | source)
XLA Modules:
  0.0 640.8 jit_solution(16056655950602185994)
XLA Ops:
  8.0 84.6 %all-gather.5.cloned.1.call-done = bf16[6144,512]{1,0:T(8,128)(2,1)} async-done(((bf16[96,512]{1,0:T(8,128)(2,1)}), bf16[6144,512]{1,0:T(8,128)(2,1)}) %all-gather.5.cloned.1.call-update) | async-done | bytes 6291472 | tf_op jit(solution)/shard_map/all_gather | solution.py:25
  92.6 95.5 %while.24 = (s32[]{:T(128)}, f32[2048]{0:T(1024)S(1)}, f32[2048]{0:T(1024)S(1)}, bf16[12,512,512]{2,1,0:T(8,128)(2,1)}, bf16[2048,512]{1,0:T(8,128)(2,1)}, /*index=5*/s32[]{:T(128)}, s32[]{:T(128)}) while((s32[]{:T(128)}, f32[2048]{0:T(1024)S(1)}, f32[2048]{0:T(1024)S(1)}, bf16[12,512,512]{2,1,0:T(8,128)(2,1)}, ...), condition=%wide.region_3.4_spmd.clone, body=%wide.region_0.3_spmd.clone.sunk | while | flops 1076897792 | bytes 11117144 | solution.py:37
  92.6 5.1 fusion.26
  97.8 2.8 exponential_reduce_fusion.2
  100.6 5.1 fusion.26
  105.7 2.8 exponential_reduce_fusion.2
  108.5 5.1 fusion.26
  113.7 2.8 exponential_reduce_fusion.2
  116.5 5.1 fusion.26
  121.6 2.8 exponential_reduce_fusion.2
  124.4 5.1 fusion.26
  129.6 2.8 exponential_reduce_fusion.2
  132.4 5.1 fusion.26
  137.5 2.8 exponential_reduce_fusion.2
  140.4 5.1 fusion.26
  145.5 2.8 exponential_reduce_fusion.2
  148.3 5.1 fusion.26
  153.5 2.8 exponential_reduce_fusion.2
  156.3 5.1 fusion.26
  161.5 2.8 exponential_reduce_fusion.2
  164.3 5.1 fusion.26
  169.4 2.8 exponential_reduce_fusion.2
  172.2 5.1 fusion.26
  177.4 2.8 exponential_reduce_fusion.2
  180.2 5.1 fusion.26
  185.3 2.8 exponential_reduce_fusion.2
  188.2 16.7 %while.25 = (s32[]{:T(128)}, f32[1536,512]{1,0:T(8,128)S(1)}, bf16[4,512,512]{2,1,0:T(8,128)(2,1)}, bf16[1536,512]{1,0:T(8,128)(2,1)}, f32[4,512]{1,0:T(4,128)S(1)}, /*index=5*/s32[]{:T(128)}, s32[]{:T(128)}) while((s32[]{:T(128)}, f32[1536,512]{1,0:T(8,128)S(1)}, bf16[4,512,512]{2,1,0:T(8,128)(2,1)}, bf16[1536,512]{1,0:T(8,128)(2,1)}, ...), condition=%wide.region_5.6_spmd.clone, body=%wide.region_4.5_spmd.clone.sunk | while | flops 1616117760 | bytes 8920155 | solution.py:53
  188.2 4.1 convolution_add_fusion.2
  192.4 4.1 convolution_add_fusion.2
  196.5 4.1 convolution_add_fusion.2
  200.7 4.1 convolution_add_fusion.2
  204.9 334.7 %fusion = f32[16,512]{1,0:T(8,128)S(1)} fusion(f32[1536,512]{1,0:T(8,128)S(1)} %get-tuple-element.62), kind=kCustom, calls=%all-reduce-scatter | all-reduce-scatter fusion | flops 1048577 | bytes 3178496
  551.3 8.4 %collective-permute-start.15 = (f32[16,512]{1,0:T(8,128)S(1)}, f32[16,512]{1,0:T(8,128)S(1)}, u32[]{:S(2)}, u32[]{:S(2)}) collective-permute-start(f32[16,512]{1,0:T(8,128)S(1)} %fusion), channel_id=1, source_target_pairs={{0,16},{1,17},{2,18},{3,19},{4,20},{5,21},{6,22},{7,23},{8,24},{9,... | collective-permute-start | bytes 98312
  559.7 6.5 %collective-permute-start.16 = (f32[16,512]{1,0:T(8,128)S(1)}, f32[16,512]{1,0:T(8,128)S(1)}, u32[]{:S(2)}, u32[]{:S(2)}) collective-permute-start(f32[16,512]{1,0:T(8,128)S(1)} %fusion), channel_id=1, source_target_pairs={{0,17},{1,18},{2,19},{3,20},{4,21},{5,22},{6,23},{7,24},{8,25},{9,... | collective-permute-start | bytes 98312
  566.2 7.1 %collective-permute-start.17 = (f32[16,512]{1,0:T(8,128)S(1)}, f32[16,512]{1,0:T(8,128)S(1)}, u32[]{:S(2)}, u32[]{:S(2)}) collective-permute-start(f32[16,512]{1,0:T(8,128)S(1)} %fusion), channel_id=1, source_target_pairs={{0,18},{1,19},{2,20},{3,21},{4,22},{5,23},{6,24},{7,25},{8,26},{9,... | collective-permute-start | bytes 98312
  573.3 4.0 collective-permute-start.18
  579.0 2.4 collective-permute-start.2
  581.5 2.0 collective-permute-start.20
  583.5 5.1 collective-permute-start.21
  593.6 2.8 collective-permute-start.25
  596.4 3.1 collective-permute-start.26
  600.9 2.3 collective-permute-start.28
  606.1 2.8 collective-permute-start.30
  610.6 6.9 %collective-permute-start.5 = (f32[16,512]{1,0:T(8,128)S(1)}, f32[16,512]{1,0:T(8,128)S(1)}, u32[]{:S(2)}, u32[]{:S(2)}) collective-permute-start(f32[16,512]{1,0:T(8,128)S(1)} %fusion), channel_id=1, source_target_pairs={{0,6},{1,7},{2,8},{3,9},{4,10},{5,11},{6,12},{7,13},{8,14},{9,15},... | collective-permute-start | bytes 98312
  619.0 2.4 collective-permute-start.7
  621.4 4.7 collective-permute-start.8
  626.2 2.1 collective-permute-start.9
  629.3 3.8 concatenate
  (105 shorter events, 29.1 us)
Async XLA Ops:
  6.5 86.1 %all-gather.5.cloned.1.call-start = ((), (), s32[]{:S(2)}) async-start(), calls=%async_computation.1 | async-start | bytes 6389760 | tf_op jit(solution)/shard_map/all_gather | solution.py:25
  7.3 180.9 %all-gather.3.cloned.1.call-start = ((), (), s32[]{:S(2)}) async-start(), calls=%async_computation | async-start | bytes 1597440 | tf_op jit(solution)/shard_map/all_gather | solution.py:40
  204.8 428.4 %copy-start = (bf16[24,512]{1,0:T(8,128)(2,1)S(1)}, bf16[24,512]{1,0:T(8,128)(2,1)}, u32[]{:S(2)}) copy-start(bf16[24,512]{1,0:T(8,128)(2,1)} %param.9) | copy-start | bytes 73732
  539.6 9.1 %collective-permute-start = (f32[16,512]{1,0:T(8,128)S(1)}, f32[16,512]{1,0:T(8,128)S(1)}, u32[]{:S(2)}, u32[]{:S(2)}) collective-permute-start(f32[16,512]{1,0:T(8,128)S(1)} %fusion), channel_id=1, source_target_pairs={{0,1},{1,2},{2,3},{3,4},{4,5},{5,6},{6,7},{7,8},{8,9},{9,10},{10,1... | collective-permute-start | bytes 98312
  541.5 5.8 collective-permute-start.31
  542.8 7.2 %collective-permute-start.1 = (f32[16,512]{1,0:T(8,128)S(1)}, f32[16,512]{1,0:T(8,128)S(1)}, u32[]{:S(2)}, u32[]{:S(2)}) collective-permute-start(f32[16,512]{1,0:T(8,128)S(1)} %fusion), channel_id=1, source_target_pairs={{0,2},{1,3},{2,4},{3,5},{4,6},{5,7},{6,8},{7,9},{8,10},{9,11},{10,... | collective-permute-start | bytes 98312
  544.7 6.5 %collective-permute-start.10 = (f32[16,512]{1,0:T(8,128)S(1)}, f32[16,512]{1,0:T(8,128)S(1)}, u32[]{:S(2)}, u32[]{:S(2)}) collective-permute-start(f32[16,512]{1,0:T(8,128)S(1)} %fusion), channel_id=1, source_target_pairs={{0,11},{1,12},{2,13},{3,14},{4,15},{5,16},{6,17},{7,18},{8,19},{9,... | collective-permute-start | bytes 98312
  546.0 13.7 %collective-permute-start.11 = (f32[16,512]{1,0:T(8,128)S(1)}, f32[16,512]{1,0:T(8,128)S(1)}, u32[]{:S(2)}, u32[]{:S(2)}) collective-permute-start(f32[16,512]{1,0:T(8,128)S(1)} %fusion), channel_id=1, source_target_pairs={{0,12},{1,13},{2,14},{3,15},{4,16},{5,17},{6,18},{7,19},{8,20},{9,... | collective-permute-start | bytes 98312
  547.3 18.9 %collective-permute-start.12 = (f32[16,512]{1,0:T(8,128)S(1)}, f32[16,512]{1,0:T(8,128)S(1)}, u32[]{:S(2)}, u32[]{:S(2)}) collective-permute-start(f32[16,512]{1,0:T(8,128)S(1)} %fusion), channel_id=1, source_target_pairs={{0,13},{1,14},{2,15},{3,16},{4,17},{5,18},{6,19},{7,20},{8,21},{9,... | collective-permute-start | bytes 98312
  548.7 24.7 %collective-permute-start.13 = (f32[16,512]{1,0:T(8,128)S(1)}, f32[16,512]{1,0:T(8,128)S(1)}, u32[]{:S(2)}, u32[]{:S(2)}) collective-permute-start(f32[16,512]{1,0:T(8,128)S(1)} %fusion), channel_id=1, source_target_pairs={{0,14},{1,15},{2,16},{3,17},{4,18},{5,19},{6,20},{7,21},{8,22},{9,... | collective-permute-start | bytes 98312
  550.0 27.3 %collective-permute-start.14 = (f32[16,512]{1,0:T(8,128)S(1)}, f32[16,512]{1,0:T(8,128)S(1)}, u32[]{:S(2)}, u32[]{:S(2)}) collective-permute-start(f32[16,512]{1,0:T(8,128)S(1)} %fusion), channel_id=1, source_target_pairs={{0,15},{1,16},{2,17},{3,18},{4,19},{5,20},{6,21},{7,22},{8,23},{9,... | collective-permute-start | bytes 98312
  551.3 27.7 %collective-permute-start.15 = (f32[16,512]{1,0:T(8,128)S(1)}, f32[16,512]{1,0:T(8,128)S(1)}, u32[]{:S(2)}, u32[]{:S(2)}) collective-permute-start(f32[16,512]{1,0:T(8,128)S(1)} %fusion), channel_id=1, source_target_pairs={{0,16},{1,17},{2,18},{3,19},{4,20},{5,21},{6,22},{7,23},{8,24},{9,... | collective-permute-start | bytes 98312
  559.7 21.8 %collective-permute-start.16 = (f32[16,512]{1,0:T(8,128)S(1)}, f32[16,512]{1,0:T(8,128)S(1)}, u32[]{:S(2)}, u32[]{:S(2)}) collective-permute-start(f32[16,512]{1,0:T(8,128)S(1)} %fusion), channel_id=1, source_target_pairs={{0,17},{1,18},{2,19},{3,20},{4,21},{5,22},{6,23},{7,24},{8,25},{9,... | collective-permute-start | bytes 98312
  566.2 17.3 %collective-permute-start.17 = (f32[16,512]{1,0:T(8,128)S(1)}, f32[16,512]{1,0:T(8,128)S(1)}, u32[]{:S(2)}, u32[]{:S(2)}) collective-permute-start(f32[16,512]{1,0:T(8,128)S(1)} %fusion), channel_id=1, source_target_pairs={{0,18},{1,19},{2,20},{3,21},{4,22},{5,23},{6,24},{7,25},{8,26},{9,... | collective-permute-start | bytes 98312
  573.3 15.3 %collective-permute-start.18 = (f32[16,512]{1,0:T(8,128)S(1)}, f32[16,512]{1,0:T(8,128)S(1)}, u32[]{:S(2)}, u32[]{:S(2)}) collective-permute-start(f32[16,512]{1,0:T(8,128)S(1)} %fusion), channel_id=1, source_target_pairs={{0,19},{1,20},{2,21},{3,22},{4,23},{5,24},{6,25},{7,26},{8,27},{9,... | collective-permute-start | bytes 98312
  577.3 13.3 %collective-permute-start.19 = (f32[16,512]{1,0:T(8,128)S(1)}, f32[16,512]{1,0:T(8,128)S(1)}, u32[]{:S(2)}, u32[]{:S(2)}) collective-permute-start(f32[16,512]{1,0:T(8,128)S(1)} %fusion), channel_id=1, source_target_pairs={{0,20},{1,21},{2,22},{3,23},{4,24},{5,25},{6,26},{7,27},{8,28},{9,... | collective-permute-start | bytes 98312
  579.0 12.9 %collective-permute-start.2 = (f32[16,512]{1,0:T(8,128)S(1)}, f32[16,512]{1,0:T(8,128)S(1)}, u32[]{:S(2)}, u32[]{:S(2)}) collective-permute-start(f32[16,512]{1,0:T(8,128)S(1)} %fusion), channel_id=1, source_target_pairs={{0,3},{1,4},{2,5},{3,6},{4,7},{5,8},{6,9},{7,10},{8,11},{9,12},{10... | collective-permute-start | bytes 98312
  581.5 12.1 %collective-permute-start.20 = (f32[16,512]{1,0:T(8,128)S(1)}, f32[16,512]{1,0:T(8,128)S(1)}, u32[]{:S(2)}, u32[]{:S(2)}) collective-permute-start(f32[16,512]{1,0:T(8,128)S(1)} %fusion), channel_id=1, source_target_pairs={{0,21},{1,22},{2,23},{3,24},{4,25},{5,26},{6,27},{7,28},{8,29},{9,... | collective-permute-start | bytes 98312
  583.5 12.9 %collective-permute-start.21 = (f32[16,512]{1,0:T(8,128)S(1)}, f32[16,512]{1,0:T(8,128)S(1)}, u32[]{:S(2)}, u32[]{:S(2)}) collective-permute-start(f32[16,512]{1,0:T(8,128)S(1)} %fusion), channel_id=1, source_target_pairs={{0,22},{1,23},{2,24},{3,25},{4,26},{5,27},{6,28},{7,29},{8,30},{9,... | collective-permute-start | bytes 98312
  588.6 11.0 %collective-permute-start.22 = (f32[16,512]{1,0:T(8,128)S(1)}, f32[16,512]{1,0:T(8,128)S(1)}, u32[]{:S(2)}, u32[]{:S(2)}) collective-permute-start(f32[16,512]{1,0:T(8,128)S(1)} %fusion), channel_id=1, source_target_pairs={{0,23},{1,24},{2,25},{3,26},{4,27},{5,28},{6,29},{7,30},{8,31},{9,... | collective-permute-start | bytes 98312
  590.6 10.3 %collective-permute-start.23 = (f32[16,512]{1,0:T(8,128)S(1)}, f32[16,512]{1,0:T(8,128)S(1)}, u32[]{:S(2)}, u32[]{:S(2)}) collective-permute-start(f32[16,512]{1,0:T(8,128)S(1)} %fusion), channel_id=1, source_target_pairs={{0,24},{1,25},{2,26},{3,27},{4,28},{5,29},{6,30},{7,31},{8,32},{9,... | collective-permute-start | bytes 98312
  591.9 11.3 %collective-permute-start.24 = (f32[16,512]{1,0:T(8,128)S(1)}, f32[16,512]{1,0:T(8,128)S(1)}, u32[]{:S(2)}, u32[]{:S(2)}) collective-permute-start(f32[16,512]{1,0:T(8,128)S(1)} %fusion), channel_id=1, source_target_pairs={{0,25},{1,26},{2,27},{3,28},{4,29},{5,30},{6,31},{7,32},{8,33},{9,... | collective-permute-start | bytes 98312
  593.6 10.9 %collective-permute-start.25 = (f32[16,512]{1,0:T(8,128)S(1)}, f32[16,512]{1,0:T(8,128)S(1)}, u32[]{:S(2)}, u32[]{:S(2)}) collective-permute-start(f32[16,512]{1,0:T(8,128)S(1)} %fusion), channel_id=1, source_target_pairs={{0,26},{1,27},{2,28},{3,29},{4,30},{5,31},{6,32},{7,33},{8,34},{9,... | collective-permute-start | bytes 98312
  596.4 9.7 %collective-permute-start.26 = (f32[16,512]{1,0:T(8,128)S(1)}, f32[16,512]{1,0:T(8,128)S(1)}, u32[]{:S(2)}, u32[]{:S(2)}) collective-permute-start(f32[16,512]{1,0:T(8,128)S(1)} %fusion), channel_id=1, source_target_pairs={{0,27},{1,28},{2,29},{3,30},{4,31},{5,32},{6,33},{7,34},{8,35},{9,... | collective-permute-start | bytes 98312
  599.6 9.3 %collective-permute-start.27 = (f32[16,512]{1,0:T(8,128)S(1)}, f32[16,512]{1,0:T(8,128)S(1)}, u32[]{:S(2)}, u32[]{:S(2)}) collective-permute-start(f32[16,512]{1,0:T(8,128)S(1)} %fusion), channel_id=1, source_target_pairs={{0,28},{1,29},{2,30},{3,31},{4,32},{5,33},{6,34},{7,35},{8,36},{9,... | collective-permute-start | bytes 98312
  600.9 9.6 %collective-permute-start.28 = (f32[16,512]{1,0:T(8,128)S(1)}, f32[16,512]{1,0:T(8,128)S(1)}, u32[]{:S(2)}, u32[]{:S(2)}) collective-permute-start(f32[16,512]{1,0:T(8,128)S(1)} %fusion), channel_id=1, source_target_pairs={{0,29},{1,30},{2,31},{3,32},{4,33},{5,34},{6,35},{7,36},{8,37},{9,... | collective-permute-start | bytes 98312
  603.2 14.3 %collective-permute-start.29 = (f32[16,512]{1,0:T(8,128)S(1)}, f32[16,512]{1,0:T(8,128)S(1)}, u32[]{:S(2)}, u32[]{:S(2)}) collective-permute-start(f32[16,512]{1,0:T(8,128)S(1)} %fusion), channel_id=1, source_target_pairs={{0,30},{1,31},{2,32},{3,33},{4,34},{5,35},{6,36},{7,37},{8,38},{9,... | collective-permute-start | bytes 98312
  604.5 14.5 %collective-permute-start.3 = (f32[16,512]{1,0:T(8,128)S(1)}, f32[16,512]{1,0:T(8,128)S(1)}, u32[]{:S(2)}, u32[]{:S(2)}) collective-permute-start(f32[16,512]{1,0:T(8,128)S(1)} %fusion), channel_id=1, source_target_pairs={{0,4},{1,5},{2,6},{3,7},{4,8},{5,9},{6,10},{7,11},{8,12},{9,13},{1... | collective-permute-start | bytes 98312
  606.1 15.3 %collective-permute-start.30 = (f32[16,512]{1,0:T(8,128)S(1)}, f32[16,512]{1,0:T(8,128)S(1)}, u32[]{:S(2)}, u32[]{:S(2)}) collective-permute-start(f32[16,512]{1,0:T(8,128)S(1)} %fusion), channel_id=1, source_target_pairs={{0,31},{1,32},{2,33},{3,34},{4,35},{5,36},{6,37},{7,38},{8,39},{9,... | collective-permute-start | bytes 98312
  608.9 17.3 %collective-permute-start.4 = (f32[16,512]{1,0:T(8,128)S(1)}, f32[16,512]{1,0:T(8,128)S(1)}, u32[]{:S(2)}, u32[]{:S(2)}) collective-permute-start(f32[16,512]{1,0:T(8,128)S(1)} %fusion), channel_id=1, source_target_pairs={{0,5},{1,6},{2,7},{3,8},{4,9},{5,10},{6,11},{7,12},{8,13},{9,14},{... | collective-permute-start | bytes 98312
  610.6 17.7 %collective-permute-start.5 = (f32[16,512]{1,0:T(8,128)S(1)}, f32[16,512]{1,0:T(8,128)S(1)}, u32[]{:S(2)}, u32[]{:S(2)}) collective-permute-start(f32[16,512]{1,0:T(8,128)S(1)} %fusion), channel_id=1, source_target_pairs={{0,6},{1,7},{2,8},{3,9},{4,10},{5,11},{6,12},{7,13},{8,14},{9,15},... | collective-permute-start | bytes 98312
  617.5 10.8 %collective-permute-start.6 = (f32[16,512]{1,0:T(8,128)S(1)}, f32[16,512]{1,0:T(8,128)S(1)}, u32[]{:S(2)}, u32[]{:S(2)}) collective-permute-start(f32[16,512]{1,0:T(8,128)S(1)} %fusion), channel_id=1, source_target_pairs={{0,7},{1,8},{2,9},{3,10},{4,11},{5,12},{6,13},{7,14},{8,15},{9,16}... | collective-permute-start | bytes 98312
  619.0 9.4 %collective-permute-start.7 = (f32[16,512]{1,0:T(8,128)S(1)}, f32[16,512]{1,0:T(8,128)S(1)}, u32[]{:S(2)}, u32[]{:S(2)}) collective-permute-start(f32[16,512]{1,0:T(8,128)S(1)} %fusion), channel_id=1, source_target_pairs={{0,8},{1,9},{2,10},{3,11},{4,12},{5,13},{6,14},{7,15},{8,16},{9,17... | collective-permute-start | bytes 98312
  621.4 6.9 %collective-permute-start.8 = (f32[16,512]{1,0:T(8,128)S(1)}, f32[16,512]{1,0:T(8,128)S(1)}, u32[]{:S(2)}, u32[]{:S(2)}) collective-permute-start(f32[16,512]{1,0:T(8,128)S(1)} %fusion), channel_id=1, source_target_pairs={{0,9},{1,10},{2,11},{3,12},{4,13},{5,14},{6,15},{7,16},{8,17},{9,1... | collective-permute-start | bytes 98312
  626.2 3.1 collective-permute-start.9
Sparse Core Ops, SparseCore 0:
  10.6 82.0 all-gather.4
  95.8 63.7 all-gather.2
where the time goes:
time: 644 us; the launch traced here: 641 us
  blocking collectives  335 us (52%)
  starting transfers between devices  88.2 us (14%)
  waiting for transfers between devices  87.1 us (14%)
  matrix products  78 us (12%)
  other arithmetic  34.5 us (5%)
  between operations  14 us (2%)
    unnamed x1, blocking collectives  335 us
    unnamed x32, starting transfers between devices  88.2 us
    all_gather x1, waiting for transfers between devices, per_device(): piece = lax.all_gather(bank, 'loop', axis=0, tiled=True)  84.6 us
    dot_general x12, matrix products, similar(): lax.dot_general(rows, columns, (((1,), (1,)), ((), ())), preferred_elemen...  61.5 us
    reduce_sum x12, other arithmetic, add_absorb(): jnp.sum(jnp.exp(scores - new_peak), axis=0)  33.4 us
    dot_general x4, matrix products, weighted_absorb(): jnp.dot(weights, block, preferred_element_type=jnp.float32)  16.5 us
  transfers between devices with their start and end apart: 34, of which 2 were waited for; matrix products, arithmetic and copies ran while one was open for 15% of the time, Pallas kernels for 0%

commit v1 on v0

v1 whole, which is shorter than its diff:
```python
import jax
import jax.numpy as jnp
from jax import lax
from jax.experimental import pallas as pl
from jax.experimental.pallas import tpu as pltpu
from jax.sharding import PartitionSpec as P

MESH = pl.DeviceIdType.MESH
SIDE = 4
STEPS = (1, 3, 2)
SLICE = 256
LOW = -1e30
CHUNK_A = {0: 0, 1: 2, 3: 3, 2: 6}
CHUNK_B = {0: 1, 1: 4, 3: 5, 2: 7}
BLOCKS = (2, 1, 3, 0)


def similar(rows, columns):
    return lax.dot_general(
        rows, columns, (((1,), (1,)), ((), ())), preferred_element_type=jnp.float32
    )


def back(distance):
    return (SIDE - distance) % SIDE


def split_rows(rows):
    half = rows.shape[2] // 2
    return jnp.concatenate([rows[:, :, :half], rows[:, :, half:]], axis=1)


def join_rows(rows):
    half = rows.shape[1] // 2
    return jnp.concatenate([rows[:, :half], rows[:, half:]], axis=2)


def kernel(
    refs, bank, queries, out,
    bank_all, own_q, gather_a, gather_b, q_all,
    peak, total, offset, scores, weights,
    pooled, from_sib, send_a, send_b, recv_a, recv_b, sum_a, sum_b, final_a, final_b,
    send_sem, recv_sem,
):
    shard, width = bank.shape
    q_rows = queries.shape[0]
    ref_count = refs.shape[0]
    chunk = 2 * SIDE * shard
    slices = ref_count // SLICE

    index, z_lo = lax.axis_index("loop"), lax.axis_index("group")
    core, y = lax.rem(index, 2), lax.rem(index // 2, SIDE)
    x, z_hi = lax.rem(index // (2 * SIDE), SIDE), index // (2 * SIDE * SIDE)

    def device(dx=0, dy=0, flip_hi=0, flip_lo=0, flip_core=0):
        to_x, to_y = lax.rem(x + dx, SIDE), lax.rem(y + dy, SIDE)
        to_hi = 1 - z_hi if flip_hi else z_hi
        to_lo = 1 - z_lo if flip_lo else z_lo
        to_core = 1 - core if flip_core else core
        return (((to_hi * SIDE + to_x) * SIDE + to_y) * 2 + to_core, to_lo)

    sibling = device(flip_core=1)
    facing = device(flip_hi=1, flip_lo=1)
    along_x = {d: device(dx=d) for d in STEPS}
    along_y = {d: device(dy=d) for d in STEPS}

    moves = {}

    def move(name, src, dst, target):
        k = len(moves)
        moves[name] = pltpu.make_async_remote_copy(
            src_ref=src, dst_ref=dst, send_sem=send_sem.at[k], recv_sem=recv_sem.at[k],
            device_id=target, device_id_type=MESH,
        )

    def bank_at(kind, line, place, count=1, side=0):
        first = (CHUNK_A if kind == "a" else CHUNK_B)[line] * chunk
        first += (side * SIDE + place) * shard
        return bank_all.at[pl.ds(first, count * shard)]

    move("bz", bank, bank_at("b", 0, 0), facing)
    first_ring = {"a": along_x, "b": along_y}
    second_ring = {"a": along_y, "b": along_x}
    gathers = {"a": gather_a, "b": gather_b}
    for kind in "ab":
        own = bank if kind == "a" else bank_at("b", 0, 0)
        for d in STEPS:
            move(f"{kind}1{d}", own, bank_at(kind, 0, back(d)), first_ring[kind][d])
        for place in range(SIDE):
            src = own if place == 0 else bank_at(kind, 0, place)
            for d in (1, 3):
                move(f"{kind}2{place}{d}", src, bank_at(kind, back(d), place), second_ring[kind][d])
        move(f"{kind}r1", bank_at(kind, 1, 0, 2), bank_at(kind, 2, 0, 2), second_ring[kind][3])
        move(f"{kind}r3", bank_at(kind, 3, 2, 2), bank_at(kind, 2, 2, 2), second_ring[kind][1])
        for line in range(SIDE):
            move(f"{kind}s{line}", bank_at(kind, line, 0, SIDE), bank_at(kind, line, 0, SIDE, 1), sibling)
    move("qz", own_q, gather_b.at[0, 0, 0], facing)
    for kind in "ab":
        gather = gathers[kind]
        own = own_q if kind == "a" else gather_b.at[0, 0, 0]
        for d in STEPS:
            move(f"q{kind}1{d}", own, gather.at[0, 0, back(d)], first_ring[kind][d])
            move(f"q{kind}2{d}", gather.at[0, 0], gather.at[back(d), 0], second_ring[kind][d])
        for line in range(SIDE):
            move(f"q{kind}s{line}", gather.at[line, 0], gather.at[line, 1], sibling)
    half = 2 * SIDE * q_rows
    for k in range(SIDE):
        move(f"ps{k}", pooled.at[k, pl.ds(half, half)], from_sib.at[k], sibling)
    for d in STEPS:
        move(f"pa{d}", send_a.at[d - 1], recv_a.at[back(d) - 1], along_y[d])
        move(f"pb{d}", send_b.at[d - 1], recv_b.at[back(d) - 1], along_x[d])
    window = 16
    same_lo = pl.ds(pl.multiple_of(8 * z_lo, 8), window)
    other_lo = pl.ds(pl.multiple_of(8 * (1 - z_lo), 8), window)
    final_devices = []
    for d in range(SIDE):
        for flip in (0, 1):
            rows = other_lo if flip else same_lo
            to_a, to_b = device(dx=d, flip_lo=flip), device(dy=d, flip_hi=1, flip_lo=flip)
            final_devices.append(to_b)
            move(f"fb{d}{flip}", sum_b.at[d, rows], final_b.at[back(d), flip], to_b)
            if d or flip:
                final_devices.append(to_a)
                move(f"fa{d}{flip}", sum_a.at[d, rows], final_a.at[back(d), flip], to_a)

    bank_all[pl.ds(CHUNK_A[0] * chunk, shard), :] = bank[...]
    peak[...] = jnp.full_like(peak, -jnp.inf)
    total[...] = jnp.zeros_like(total)
    scores[1] = jnp.full(scores.shape[1:], LOW, jnp.float32)
    own_q[...] = split_rows(queries[...].astype(jnp.float32)[None])[0].astype(jnp.bfloat16)
    gather_a[0, 0, 0] = own_q[...]

    partners = [sibling, *along_y.values(), *final_devices]
    barrier = pltpu.get_barrier_semaphore()
    for partner in partners:
        pl.semaphore_signal(barrier, inc=1, device_id=partner, device_id_type=MESH)
    pl.semaphore_wait(barrier, len(partners))

    def start(*names):
        for name in names:
            moves[name].start()

    def arrived(*names):
        for name in names:
            moves[name].wait_recv()

    def at_start():
        start("bz", "a11", "a13", "a12", "a201", "a203")
        arrived("bz")
        start("b11", "b13", "b12", "b201", "b203")
        for d in STEPS:
            arrived(f"a1{d}")
            start(f"a2{back(d)}1", f"a2{back(d)}3")
        start("as0")
        for d in STEPS:
            arrived(f"b1{d}")
            start(f"b2{back(d)}1", f"b2{back(d)}3")
        start("bs0")
        start("qz", "qa11", "qa13", "qa12")
        arrived("as0")

    def pass_on(kind, line):
        arrived(*[f"{kind}2{place}{back(line)}" for place in range(SIDE)])
        start(f"{kind}r{line}", f"{kind}s{line}")

    def before_b0():
        arrived("bs0")
        arrived("qz")
        start("qb11", "qb13", "qb12")

    def before_a1():
        pass_on("a", 1)
        pass_on("a", 3)
        pass_on("b", 1)
        pass_on("b", 3)
        arrived("qa11", "qa13", "qa12")
        start("qa21", "qa23", "qa22", "qas0")
        arrived("qb11", "qb13", "qb12")
        start("qb21", "qb23", "qb22", "qbs0")
        arrived("as1")

    def before_b3():
        arrived("bs3")
        arrived("ar1", "ar3")
        start("as2")
        arrived("br1", "br3")
        start("bs2")

    def before_a2():
        arrived("as2")
        for d in STEPS:
            arrived(f"qa2{d}", f"qb2{d}")
            start(f"qas{back(d)}", f"qbs{back(d)}")

    events = (
        at_start, before_b0, before_a1, lambda: arrived("as3"), lambda: arrived("bs1"),
        before_b3, before_a2, lambda: arrived("bs2"),
    )

    def absorb(slot, piece):
        tile = scores[slot].reshape(chunk // 8, 8, SLICE)
        columns = slice(piece * SLICE, (piece + 1) * SLICE)
        old = peak[:, columns]
        new = jnp.maximum(old, jnp.max(tile, axis=0))
        added = jnp.sum(jnp.exp(tile - new[None]), axis=0)
        total[:, columns] = total[:, columns] * jnp.exp(old - new) + added
        peak[:, columns] = new

    def one_chunk(i, carry):
        for k, event in enumerate(events):
            pl.when(i == k)(event)
        rows = pl.ds(pl.multiple_of(i * chunk, chunk), chunk)
        for piece in range(slices):
            scores[piece % 2] = similar(bank_all[rows, :], refs[piece * SLICE:(piece + 1) * SLICE, :])
            absorb((piece + 1) % 2, (piece - 1) % slices)
        return carry

    lax.fori_loop(0, len(events), one_chunk, 0)
    absorb((slices - 1) % 2, slices - 1)
    highest = jnp.max(peak[...], axis=0, keepdims=True)
    summed = jnp.sum(total[...] * jnp.exp(peak[...] - highest), axis=0, keepdims=True)
    offset[...] = jnp.broadcast_to(highest + jnp.log(summed), offset.shape)

    for d in range(SIDE):
        arrived(f"qas{d}", f"qbs{d}")
    quarter = SIDE * q_rows
    for k, line in enumerate(BLOCKS):
        for j, gather in enumerate((gather_a, gather_b)):
            for side in range(2):
                rows = join_rows(gather[line, side].astype(jnp.float32))
                first = (2 * side + j) * quarter
                q_all[k, first:first + quarter, :] = rows.reshape(quarter, width).astype(jnp.bfloat16)

    def pool(k, carry):
        block = q_all[k]
        for piece in range(slices):
            columns = slice(piece * SLICE, (piece + 1) * SLICE)
            tile = similar(block, refs[columns, :]).reshape(2 * half // 8, 8, SLICE)
            tile = 1.0 / (1.0 + jnp.exp(offset[:, columns][None] - tile))
            weights[:, columns] = tile.reshape(2 * half, SLICE).astype(jnp.bfloat16)
        pooled[k] = jnp.dot(weights[...], refs[...], preferred_element_type=jnp.float32)
        for j in range(SIDE):
            pl.when(k == j)(lambda j=j: after_pool(j))
        return carry

    def after_pool(k):
        start(f"ps{k}")
        if k >= 1:
            reduce_block(k - 1)

    def reduce_block(k):
        arrived(f"ps{k}")
        sums = pooled[k, :half, :] + from_sib[k]
        line = BLOCKS[k]
        for j, send in enumerate((send_a, send_b)):
            rows = sums[j * quarter:(j + 1) * quarter].reshape(SIDE, q_rows, width)
            send[line - 1] = split_rows(rows).astype(jnp.bfloat16)
        start(f"pa{line}", f"pb{line}")

    lax.fori_loop(0, SIDE, pool, 0)
    last = SIDE - 1
    arrived(f"ps{last}")
    sums = pooled[last, :half, :] + from_sib[last]
    for j, (name, recv, result) in enumerate((("pa", recv_a, sum_a), ("pb", recv_b, sum_b))):
        rows = sums[j * quarter:(j + 1) * quarter].reshape(SIDE, q_rows, width)
        for d in STEPS:
            arrived(f"{name}{d}")
            rows = rows + join_rows(recv[back(d) - 1].astype(jnp.float32))
        result[...] = rows
    sends = [name for name in moves if name.startswith("f")]
    start(*sends)
    rows = sum_a[0, same_lo, :]
    own = jnp.where(z_lo == 0, queries[...].astype(jnp.float32)[:window], queries[...].astype(jnp.float32)[8:])
    for name in sends:
        arrived(name)
        kind, d, flip = name[1], int(name[2]), int(name[3])
        rows = rows + (final_a if kind == "a" else final_b)[back(d), flip]
    scale = lax.rsqrt(jnp.mean(rows * rows, axis=1, keepdims=True) + 1e-06)
    result = own + rows * scale
    count = out.shape[0]
    out[...] = jnp.where(z_lo == 0, result[:count], result[window - count:])
    for copy in moves.values():
        copy.wait_send()


MOVES = 180


def per_device(references, bank, queries):
    ref_count, width = references.shape
    shard, q_rows = bank.shape[0], queries.shape[0]
    chunk = 2 * SIDE * shard
    block = 4 * SIDE * q_rows
    unit = (2 * q_rows, width // 2)
    f32, bf16 = jnp.float32, jnp.bfloat16
    return pl.pallas_call(
        kernel,
        out_shape=jax.ShapeDtypeStruct((q_rows // 2, width), f32),
        in_specs=[pl.BlockSpec(memory_space=pltpu.VMEM)] * 3,
        out_specs=pl.BlockSpec(memory_space=pltpu.VMEM),
        scratch_shapes=[
            pltpu.VMEM((2 * SIDE * chunk, width), bf16),
            pltpu.VMEM(unit, bf16),
            pltpu.VMEM((SIDE, 2, SIDE, *unit), bf16),
            pltpu.VMEM((SIDE, 2, SIDE, *unit), bf16),
            pltpu.VMEM((SIDE, block, width), bf16),
            pltpu.VMEM((8, ref_count), f32),
            pltpu.VMEM((8, ref_count), f32),
            pltpu.VMEM((8, ref_count), f32),
            pltpu.VMEM((2, chunk, SLICE), f32),
            pltpu.VMEM((block, ref_count), bf16),
            pltpu.VMEM((SIDE, block, width), f32),
            pltpu.VMEM((SIDE, block // 2, width), f32),
            pltpu.VMEM((SIDE - 1, SIDE, *unit), bf16),
            pltpu.VMEM((SIDE - 1, SIDE, *unit), bf16),
            pltpu.VMEM((SIDE - 1, SIDE, *unit), bf16),
            pltpu.VMEM((SIDE - 1, SIDE, *unit), bf16),
            pltpu.VMEM((SIDE, q_rows, width), f32),
            pltpu.VMEM((SIDE, q_rows, width), f32),
            pltpu.VMEM((SIDE, 2, 16, width), f32),
            pltpu.VMEM((SIDE, 2, 16, width), f32),
            pltpu.SemaphoreType.DMA((MOVES,)),
            pltpu.SemaphoreType.DMA((MOVES,)),
        ],
        compiler_params=pltpu.CompilerParams(
            collective_id=0, has_side_effects=True, vmem_limit_bytes=56 * 2**20
        ),
    )(references, bank, queries)


def solution(mesh):
    return jax.shard_map(
        per_device,
        mesh=mesh,
        in_specs=(P(("loop", "group"), None), P("loop", None), P("loop", None)),
        out_specs=P(("loop", "group"), None),
        check_vma=False,
    )
```

time: 644 us -> 67.7 us (0.11)
  blocking collectives: 335 us -> 0 us
  starting transfers between devices: 88.2 us -> 0 us
  waiting for transfers between devices: 87.1 us -> 0 us
  matrix products: 78 us -> 0 us
  Pallas kernels: 0 us -> 66.1 us
  other arithmetic: 34.5 us -> 0 us
  between operations: 14 us -> 0.01 us
    unnamed x1 -> x0, blocking collectives: 335 us -> none
    unnamed x32 -> x0, starting transfers between devices: 88.2 us -> none
    all_gather x2 -> x0, waiting for transfers between devices: 84.6 us -> none  [the longest x1 84.6 us: per_device(): piece = lax.all_gather(bank, 'loop', axis=0, tiled=True)]
    dot_general x16 -> x0, matrix products: 78 us -> none  [the longest x12 61.5 us: similar(): lax.dot_general(rows, columns, (((1,), (1,)), ((), ())), preferred_elemen...]
    pallas_call x0 -> x1, Pallas kernels: none -> 66.1 us  [per_device(): pl.pallas_call(kernel, out_shape=jax.ShapeDtypeStruct((q_rows // 2, width...]
    reduce_sum x13 -> x0, other arithmetic: 33.6 us -> none  [the longest x12 33.4 us: add_absorb(): jnp.sum(jnp.exp(scores - new_peak), axis=0)]
  transfers between devices with their start and end apart: 34 -> 0, of which waited for: 2 -> 0; matrix products, arithmetic and copies ran while one was open for 15% -> 0% of each run, Pallas kernels for 0% -> 0%
where the time goes in v1:
time: 67.7 us; the launch traced here: 67.5 us
  Pallas kernels  66.1 us (98%)
  local copies, waits for them, and re-layouts  1.38 us (2%)
    pallas_call x1, Pallas kernels, per_device(): pl.pallas_call(kernel, out_shape=jax.ShapeDtypeStruct((q_rows // 2, width...  66.1 us
    unnamed x1, local copies, waits for them, and re-layouts  1.38 us

profile of v1, /device:TPU:1, one launch (start us, length us, event | category | flops | bytes accessed | tf_op | source)
XLA Modules:
  0.0 67.5 jit_solution(13009414939344463826)
XLA Ops:
  0.0 66.1 %shard_map.37 = f32[12,512]{1,0:T(8,128)} custom-call(bf16[2048,512]{1,0:T(8,128)(2,1)} %refs.1, bf16[96,512]{1,0:T(8,128)(2,1)} %bank.1, bf16[24,512]{1,0:T(8,128)(2,1)} %queries.1), custom_call_target="tpu_custom_call" | custom-call | tf_op jit(solution)/shard_map/pallas_call | solution.py:296
  66.1 1.4 %copy.5 = f32[12,512]{1,0:T(8,128)} copy(f32[12,512]{1,0:T(8,128)} %shard_map.37) | data formatting | bytes 49152

commit v2 on v1

v2 whole, which is shorter than its diff:
```python
import jax
import jax.numpy as jnp
from jax import lax
from jax.experimental import pallas as pl
from jax.experimental.pallas import tpu as pltpu
from jax.sharding import PartitionSpec as P

MESH = pl.DeviceIdType.MESH
SIDE = 4
STEPS = (1, 3, 2)
SLICE = 256
LOW = -1e30
BLOCKS = (2, 1, 3, 0)


def similar(rows, columns):
    return lax.dot_general(
        rows, columns, (((1,), (1,)), ((), ())), preferred_element_type=jnp.float32
    )


def back(distance):
    return (SIDE - distance) % SIDE


def split_rows(rows):
    half = rows.shape[2] // 2
    return jnp.concatenate([rows[:, :, :half], rows[:, :, half:]], axis=1)


def join_rows(rows):
    half = rows.shape[1] // 2
    return jnp.concatenate([rows[:, :half], rows[:, half:]], axis=2)


PARTS = (
    ("a00", "b00", "a10", "a30"),
    ("a01", "a03", "b01", "b03"),
    ("a20", "b02", "b10", "b30"),
    ("a11", "a13", "b11", "b31"),
    ("a02", "b20", "near a2", "near b2"),
    ("a31", "a33", "b13", "b33"),
    ("a21", "a23", "b12", "b32"),
    ("a22", "b22", "far a2", "far b2"),
)
SLOTS = {name: (k, j) for k, names in enumerate(PARTS) for j, name in enumerate(names)}
UNITS = 4
WINDOW = 16
SEND_SEMS, RECV_SEMS = 12, 40


def kernel(
    refs_hbm, bank, queries, out,
    refs, bank_all, own_q, gather_a, gather_b, q_all,
    peak, total, offset, scores, weights,
    pooled, from_sib, send_a, send_b, recv_a, recv_b, sums, windows, final,
    load_sem, send_sem, recv_sem,
):
    shard, width = bank.shape
    q_rows = queries.shape[0]
    ref_count = refs.shape[0]
    part = UNITS * shard
    chunk = 2 * part
    slices = ref_count // SLICE

    load = pltpu.make_async_copy(refs_hbm, refs, load_sem)
    load.start()

    index, z_lo = lax.axis_index("loop"), lax.axis_index("group")
    core, y = lax.rem(index, 2), lax.rem(index // 2, SIDE)
    x, z_hi = lax.rem(index // (2 * SIDE), SIDE), index // (2 * SIDE * SIDE)

    def device(dx=0, dy=0, flip_hi=0, flip_lo=0, flip_core=0):
        to_x, to_y = lax.rem(x + dx, SIDE), lax.rem(y + dy, SIDE)
        to_hi = 1 - z_hi if flip_hi else z_hi
        to_lo = 1 - z_lo if flip_lo else z_lo
        to_core = 1 - core if flip_core else core
        return (((to_hi * SIDE + to_x) * SIDE + to_y) * 2 + to_core, to_lo)

    sibling = device(flip_core=1)
    twin = device(flip_lo=1)
    facing = device(flip_hi=1, flip_lo=1)
    along_x = {d: device(dx=d) for d in STEPS}
    along_y = {d: device(dy=d) for d in STEPS}

    moves, send_groups, recv_groups = {}, {}, {}

    def group_sem(sems, groups, name):
        return sems.at[groups.setdefault(name, len(groups))]

    def copy(src, dst, sent, landed, target):
        return pltpu.make_async_remote_copy(
            src_ref=src, dst_ref=dst,
            send_sem=group_sem(send_sem, send_groups, sent), recv_sem=group_sem(recv_sem, recv_groups, landed),
            device_id=target, device_id_type=MESH,
        )

    def move(name, src, dst, sent, landed, target):
        moves[name] = lambda: copy(src, dst, sent, landed, target)

    def start(*names):
        for name in names:
            moves[name]().start()

    def arrived(landed, what):
        copy(what, what, next(iter(send_groups)), landed, sibling).wait_recv()

    def all_sent(sent, what):
        copy(what, what, sent, next(iter(recv_groups)), sibling).wait_send()

    def first_row(k, side=0):
        return min((k + 1) * chunk, len(PARTS) * chunk - part) if side else max(k * chunk - part, 0)

    def unit(name):
        k, j = SLOTS[name]
        return bank_all.at[pl.ds(first_row(k) + j * shard, shard)]

    def whole_part(k, side=0):
        return bank_all.at[pl.ds(first_row(k, side), part)]

    def pair(name):
        k, j = SLOTS[name]
        return bank_all.at[pl.ds(first_row(k) + j * shard, 2 * shard)]

    unit_sends = []

    def send_unit(name, src, dst, landed, target):
        move(name, src, unit(dst), f"u{len(unit_sends) // 16}", landed, target)
        unit_sends.append(name)

    send_unit("z", bank, "b00", "z", facing)
    for d in STEPS:
        send_unit(f"a1{d}", bank, f"a{back(d)}0", f"a1{d}", along_x[d])
        send_unit(f"b1{d}", unit("b00"), f"b0{back(d)}", f"b1{d}", along_y[d])
    for place, k_a, k_b in ((0, 1, 2), (1, 3, 3), (3, 5, 5), (2, 6, 6)):
        for d in (1, 3):
            send_unit(f"a2{place}{d}", unit(f"a{place}0") if place else bank, f"a{place}{back(d)}", f"c{k_a}", along_y[d])
            send_unit(f"b2{place}{d}", unit(f"b0{place}"), f"b{back(d)}{place}", f"c{k_b}", along_x[d])

    def near(names):
        k, j = SLOTS[names[0]]
        return bank_all.at[pl.ds(pl.multiple_of(first_row(k) + (j + z_lo) * shard, shard), shard)]

    send_unit("a2n", near(("a10", "a30")), "near a2", "c4", along_y[2])
    send_unit("b2n", near(("b01", "b03")), "near b2", "c4", along_x[2])
    send_unit("za", unit("b02"), "a02", "c4", facing)
    send_unit("zb", unit("a20"), "b20", "c4", facing)
    send_unit("a222", unit("a20"), "a22", "c7", along_y[2])
    send_unit("b222", unit("b02"), "b22", "c7", along_x[2])
    send_unit("ta", unit("near a2"), "far a2", "c7", twin)
    send_unit("tb", unit("near b2"), "far b2", "c7", twin)
    for k in range(len(PARTS)):
        move(f"s{k}", whole_part(k), whole_part(k, 1), f"s{k // 4}", f"s{k}", sibling)

    first_ring = {"a": along_x, "b": along_y}
    second_ring = {"a": along_y, "b": along_x}
    gathers = {"a": gather_a, "b": gather_b}
    plane = SIDE * SIDE
    move("qz", own_q, gather_b.at[0], "q", "qz", facing)
    for kind, gather in gathers.items():
        own = own_q if kind == "a" else gather_b.at[0]
        for d in STEPS:
            move(f"q{kind}1{d}", own, gather.at[back(d)], "q", f"q{kind}1", first_ring[kind][d])
            move(f"q{kind}2{d}", gather.at[pl.ds(0, SIDE)], gather.at[pl.ds(back(d) * SIDE, SIDE)], "q", f"q{kind}2",
                 second_ring[kind][d])
        for name, first, count in (("0", 0, SIDE), ("3", SIDE, plane - SIDE)):
            move(f"q{kind}s{name}", gather.at[pl.ds(first, count)], gather.at[pl.ds(plane + first, count)], "qs",
                 f"q{kind}s{name}", sibling)

    half = 2 * SIDE * q_rows
    for k in range(SIDE):
        move(f"p{k}", pooled.at[k, pl.ds(half, half)], from_sib.at[k], "p", f"p{k}", sibling)
    for d in STEPS:
        move(f"pa{d}", send_a.at[d - 1], recv_a.at[back(d) - 1], "pa", "pa", along_y[d])
        move(f"pb{d}", send_b.at[d - 1], recv_b.at[back(d) - 1], "pb", "pb", along_x[d])
    ends = []
    for d in range(SIDE):
        for flip in (0, 1):
            for j, target in enumerate((device(dx=d, flip_lo=flip), device(dy=d, flip_hi=1, flip_lo=flip))):
                if d or flip or j:
                    place = (flip * 2 + j) * SIDE
                    move(f"f{place + d}", windows.at[place + d], final.at[place + back(d)], "f", "f", target)
                    ends.append(f"f{place + d}")

    bank_all[pl.ds(0, shard), :] = bank[...]
    peak[...] = jnp.full_like(peak, -jnp.inf)
    total[...] = jnp.zeros_like(total)
    scores[1] = jnp.full(scores.shape[1:], LOW, jnp.float32)
    own_q[...] = split_rows(queries[...].astype(jnp.float32)[None])[0].astype(jnp.bfloat16)
    gather_a[0] = own_q[...]

    partners = [sibling, twin, facing, device(flip_hi=1), *along_x.values(), *along_y.values()]
    barrier = pltpu.get_barrier_semaphore()
    for partner in partners:
        pl.semaphore_signal(barrier, inc=1, device_id=partner, device_id_type=MESH)
    pl.semaphore_wait(barrier, len(partners))

    def from_own(k):
        arrived(f"c{k}", whole_part(k))
        start(f"s{k}")

    def from_other(k):
        arrived(f"s{k}", whole_part(k, 1))

    def before_1():
        for d, place in ((1, 3), (3, 1)):
            arrived(f"b1{d}", unit(f"b0{place}"))
        start("a211", "a213", "b211", "b213")
        arrived("a12", unit("a20"))
        start("zb")
        arrived("c1", pair("a01"))
        start("s1", "qz")
        from_other(0)

    def before_2():
        arrived("b12", unit("b02"))
        start("a2n", "b2n", "za")
        arrived("c2", pair("b10"))
        start("s2", "qa11", "qa13", "qa12")
        from_other(1)

    def before_3():
        start("a231", "a233", "b231", "b233")
        from_own(3)
        arrived("qz", gather_b.at[0])
        start("qb11", "qb13", "qb12")
        from_other(2)

    def before_4():
        from_own(4)
        start("a221", "a223", "b221", "b223", "ta", "tb")
        from_other(3)

    def before_5():
        start("a222", "b222")
        from_own(5)
        arrived("qa1", gather_a.at[pl.ds(1, SIDE - 1)])
        arrived("qb1", gather_b.at[pl.ds(1, SIDE - 1)])
        start("qa22", "qb22", "qas0", "qbs0")
        from_other(4)

    def before_6():
        start("qa21", "qa23", "qb21", "qb23")
        from_own(6)
        from_other(5)

    def before_7():
        from_own(7)
        from_other(6)

    events = (before_1, before_2, before_3, before_4, before_5, before_6, before_7)

    def absorb(slot, piece, count=chunk):
        tile = scores[slot, :count].reshape(count // 8, 8, SLICE)
        columns = slice(piece * SLICE, (piece + 1) * SLICE)
        old = peak[:, columns]
        new = jnp.maximum(old, jnp.max(tile, axis=0))
        added = jnp.sum(jnp.exp(tile - new[None]), axis=0)
        total[:, columns] = total[:, columns] * jnp.exp(old - new) + added
        peak[:, columns] = new

    def score(first, count, before=chunk):
        rows = pl.ds(first, count)
        for piece in range(slices):
            scores[piece % 2, :count] = similar(bank_all[rows, :], refs[piece * SLICE:(piece + 1) * SLICE, :])
            absorb((piece + 1) % 2, (piece - 1) % slices, count if piece else before)

    start("z", "a11", "a13", "a201", "a203", "a12")
    arrived("z", unit("b00"))
    start("b11", "b13")
    for d, place in ((1, 3), (3, 1)):
        arrived(f"a1{d}", unit(f"a{place}0"))
    start("b201", "b203", "b12", "s0")
    load.wait()
    score(0, part)

    def one_chunk(i, carry):
        for k, event in enumerate(events):
            pl.when(i == k)(event)
        score(pl.multiple_of(part + i * chunk, part), chunk)
        return carry

    lax.fori_loop(0, len(events), one_chunk, 0)
    rest = pl.ds(SIDE, plane - SIDE)
    for kind, gather in gathers.items():
        arrived(f"q{kind}2", gather.at[rest])
        start(f"q{kind}s3")
    from_other(len(PARTS) - 1)
    score(first_row(len(PARTS) - 1, 1), part)
    absorb((slices - 1) % 2, slices - 1, part)
    highest = jnp.max(peak[...], axis=0, keepdims=True)
    summed = jnp.sum(total[...] * jnp.exp(peak[...] - highest), axis=0, keepdims=True)
    offset[...] = jnp.broadcast_to(highest + jnp.log(summed), offset.shape)

    quarter = SIDE * q_rows
    for kind, gather in gathers.items():
        arrived(f"q{kind}s0", gather.at[pl.ds(plane, SIDE)])
        arrived(f"q{kind}s3", gather.at[pl.ds(plane + SIDE, plane - SIDE)])
    for k, line in enumerate(BLOCKS):
        for j, gather in enumerate((gather_a, gather_b)):
            for side in range(2):
                first = side * plane + line * SIDE
                rows = join_rows(gather[first:first + SIDE].astype(jnp.float32))
                first = (2 * side + j) * quarter
                q_all[k, first:first + quarter, :] = rows.reshape(quarter, width).astype(jnp.bfloat16)

    def pool(k, carry):
        block = q_all[k]
        for piece in range(slices):
            columns = slice(piece * SLICE, (piece + 1) * SLICE)
            tile = similar(block, refs[columns, :]).reshape(2 * half // 8, 8, SLICE)
            tile = 1.0 / (1.0 + jnp.exp(offset[:, columns][None] - tile))
            weights[:, columns] = tile.reshape(2 * half, SLICE).astype(jnp.bfloat16)
        pooled[k] = jnp.dot(weights[...], refs[...], preferred_element_type=jnp.float32)
        for j in range(SIDE):
            pl.when(k == j)(lambda j=j: after_pool(j))
        return carry

    def after_pool(k):
        start(f"p{k}")
        if k >= 1:
            reduce_block(k - 1)

    def both_cores(k):
        arrived(f"p{k}", from_sib.at[k])
        rows = pooled[k, :half, :] + from_sib[k]
        return [rows[j * quarter:(j + 1) * quarter].reshape(SIDE, q_rows, width) for j in range(2)]

    def reduce_block(k):
        line = BLOCKS[k]
        for rows, send in zip(both_cores(k), (send_a, send_b)):
            send[line - 1] = split_rows(rows).astype(jnp.bfloat16)
        start(f"pa{line}", f"pb{line}")

    lax.fori_loop(0, SIDE, pool, 0)
    same_lo = pl.ds(pl.multiple_of(8 * z_lo, 8), WINDOW)
    other_lo = pl.ds(pl.multiple_of(8 * (1 - z_lo), 8), WINDOW)
    for j, (rows, recv) in enumerate(zip(both_cores(SIDE - 1), (recv_a, recv_b))):
        arrived("pa" if j == 0 else "pb", recv)
        sums[j] = rows + sum(join_rows(recv[d].astype(jnp.float32)) for d in range(SIDE - 1))
        for flip, lo in enumerate((same_lo, other_lo)):
            first = (flip * 2 + j) * SIDE
            windows[first:first + SIDE] = sums[j, :, lo, :].astype(jnp.bfloat16)
    start(*ends)
    rows = sums[0, 0, same_lo, :]
    own = queries[...].astype(jnp.float32)
    own = jnp.where(z_lo == 0, own[:WINDOW], own[q_rows - WINDOW:])
    arrived("f", final.at[pl.ds(1, 4 * SIDE - 1)])
    rows = rows + jnp.sum(final[1:].astype(jnp.float32), axis=0)
    scale = lax.rsqrt(jnp.mean(rows * rows, axis=1, keepdims=True) + 1e-06)
    result = own + rows * scale
    count = out.shape[0]
    out[...] = jnp.where(z_lo == 0, result[:count], result[WINDOW - count:])

    all_sent("u0", bank_all.at[pl.ds(0, 16 * shard)])
    all_sent("u1", bank_all.at[pl.ds(0, (len(unit_sends) - 16) * shard)])
    all_sent("s0", bank_all.at[pl.ds(0, 4 * part)])
    all_sent("s1", bank_all.at[pl.ds(0, 4 * part)])
    all_sent("q", gather_a.at[pl.ds(0, 2 * plane - 1)])
    all_sent("qs", gather_a)
    all_sent("p", from_sib)
    all_sent("pa", send_a)
    all_sent("pb", send_b)
    all_sent("f", final.at[pl.ds(1, 4 * SIDE - 1)])


def per_device(references, bank, queries):
    ref_count, width = references.shape
    shard, q_rows = bank.shape[0], queries.shape[0]
    chunk = 2 * UNITS * shard
    block = 4 * SIDE * q_rows
    unit = (2 * q_rows, width // 2)
    f32, bf16 = jnp.float32, jnp.bfloat16
    return pl.pallas_call(
        kernel,
        out_shape=jax.ShapeDtypeStruct((q_rows // 2, width), f32),
        in_specs=[
            pl.BlockSpec(memory_space=pl.ANY),
            pl.BlockSpec(memory_space=pltpu.VMEM),
            pl.BlockSpec(memory_space=pltpu.VMEM),
        ],
        out_specs=pl.BlockSpec(memory_space=pltpu.VMEM),
        scratch_shapes=[
            pltpu.VMEM((ref_count, width), bf16),
            pltpu.VMEM((len(PARTS) * chunk, width), bf16),
            pltpu.VMEM(unit, bf16),
            pltpu.VMEM((2 * SIDE * SIDE, *unit), bf16),
            pltpu.VMEM((2 * SIDE * SIDE, *unit), bf16),
            pltpu.VMEM((SIDE, block, width), bf16),
            pltpu.VMEM((8, ref_count), f32),
            pltpu.VMEM((8, ref_count), f32),
            pltpu.VMEM((8, ref_count), f32),
            pltpu.VMEM((2, chunk, SLICE), f32),
            pltpu.VMEM((block, ref_count), bf16),
            pltpu.VMEM((SIDE, block, width), f32),
            pltpu.VMEM((SIDE, block // 2, width), f32),
            pltpu.VMEM((SIDE - 1, SIDE, *unit), bf16),
            pltpu.VMEM((SIDE - 1, SIDE, *unit), bf16),
            pltpu.VMEM((SIDE - 1, SIDE, *unit), bf16),
            pltpu.VMEM((SIDE - 1, SIDE, *unit), bf16),
            pltpu.VMEM((2, SIDE, q_rows, width), f32),
            pltpu.VMEM((4 * SIDE, WINDOW, width), bf16),
            pltpu.VMEM((4 * SIDE, WINDOW, width), bf16),
            pltpu.SemaphoreType.DMA,
            pltpu.SemaphoreType.DMA((SEND_SEMS,)),
            pltpu.SemaphoreType.DMA((RECV_SEMS,)),
        ],
        compiler_params=pltpu.CompilerParams(
            collective_id=0, has_side_effects=True, vmem_limit_bytes=56 * 2**20
        ),
    )(references, bank, queries)


def solution(mesh):
    return jax.shard_map(
        per_device,
        mesh=mesh,
        in_specs=(P(("loop", "group"), None), P("loop", None), P("loop", None)),
        out_specs=P(("loop", "group"), None),
        check_vma=False,
    )
```

time: 67.7 us -> 61.1 us (0.903)
  Pallas kernels: 66.1 us -> 59.5 us
    pallas_call x1, Pallas kernels: 66.1 us -> 59.5 us  [per_device(): pl.pallas_call(kernel, out_shape=jax.ShapeDtypeStruct((q_rows // 2, width...]
where the time goes in v2:
time: 61.1 us; the launch traced here: 60.9 us
  Pallas kernels  59.5 us (97%)
  local copies, waits for them, and re-layouts  1.38 us (2%)
    pallas_call x1, Pallas kernels, per_device(): pl.pallas_call(kernel, out_shape=jax.ShapeDtypeStruct((q_rows // 2, width...  59.5 us
    unnamed x1, local copies, waits for them, and re-layouts  1.38 us

profile of v2, /device:TPU:1, one launch (start us, length us, event | category | flops | bytes accessed | tf_op | source)
XLA Modules:
  0.0 60.9 jit_solution(1000417434762663996)
XLA Ops:
  0.0 59.5 %shard_map.37 = f32[12,512]{1,0:T(8,128)} custom-call(bf16[2048,512]{1,0:T(8,128)(2,1)} %refs_hbm.1, bf16[96,512]{1,0:T(8,128)(2,1)} %bank.1, bf16[24,512]{1,0:T(8,128)(2,1)} %queries.1), custom_call_target="tpu_custom_call" | custom-call | tf_op jit(solution)/shard_map/pallas_call | solution.py:374
  59.5 1.4 %copy.5 = f32[12,512]{1,0:T(8,128)} copy(f32[12,512]{1,0:T(8,128)} %shard_map.37) | data formatting | bytes 49152

commit v3 on v2

--- a/solution.py
+++ b/solution.py
@@ -205,7 +205,7 @@
     def before_1():
         for d, place in ((1, 3), (3, 1)):
             arrived(f"b1{d}", unit(f"b0{place}"))
-        start("a211", "a213", "b211", "b213")
+        start("a211", "a213", "b211", "b213", "a2n", "b2n", "a231", "a233", "b231", "b233")
         arrived("a12", unit("a20"))
         start("zb")
         arrived("c1", pair("a01"))
@@ -214,13 +214,12 @@
 
     def before_2():
         arrived("b12", unit("b02"))
-        start("a2n", "b2n", "za")
+        start("za")
         arrived("c2", pair("b10"))
-        start("s2", "qa11", "qa13", "qa12")
+        start("s2", "qa11", "qa13", "qa12", "a221", "a223", "b221", "b223")
         from_other(1)
 
     def before_3():
-        start("a231", "a233", "b231", "b233")
         from_own(3)
         arrived("qz", gather_b.at[0])
         start("qb11", "qb13", "qb12")
@@ -228,11 +227,10 @@
 
     def before_4():
         from_own(4)
-        start("a221", "a223", "b221", "b223", "ta", "tb")
+        start("ta", "tb", "a222", "b222")
         from_other(3)
 
     def before_5():
-        start("a222", "b222")
         from_own(5)
         arrived("qa1", gather_a.at[pl.ds(1, SIDE - 1)])
         arrived("qb1", gather_b.at[pl.ds(1, SIDE - 1)])

time: 61.1 us -> 57.9 us (0.948)
  Pallas kernels: 59.5 us -> 56.3 us
    pallas_call x1, Pallas kernels: 59.5 us -> 56.3 us  [per_device(): pl.pallas_call(kernel, out_shape=jax.ShapeDtypeStruct((q_rows // 2, width...]
where the time goes in v3:
time: 57.9 us; the launch traced here: 57.7 us
  Pallas kernels  56.3 us (97%)
  local copies, waits for them, and re-layouts  1.38 us (2%)
    pallas_call x1, Pallas kernels, per_device(): pl.pallas_call(kernel, out_shape=jax.ShapeDtypeStruct((q_rows // 2, width...  56.3 us
    unnamed x1, local copies, waits for them, and re-layouts  1.38 us

profile of v3, /device:TPU:1, one launch (start us, length us, event | category | flops | bytes accessed | tf_op | source)
XLA Modules:
  0.0 57.7 jit_solution(4782881458374276804)
XLA Ops:
  0.0 56.3 %shard_map.37 = f32[12,512]{1,0:T(8,128)} custom-call(bf16[2048,512]{1,0:T(8,128)(2,1)} %refs_hbm.1, bf16[96,512]{1,0:T(8,128)(2,1)} %bank.1, bf16[24,512]{1,0:T(8,128)(2,1)} %queries.1), custom_call_target="tpu_custom_call" | custom-call | tf_op jit(solution)/shard_map/pallas_call | solution.py:372
  56.3 1.4 %copy.5 = f32[12,512]{1,0:T(8,128)} copy(f32[12,512]{1,0:T(8,128)} %shard_map.37) | data formatting | bytes 49152

commit v4 on v3

--- a/solution.py
+++ b/solution.py
@@ -10,7 +10,7 @@
 STEPS = (1, 3, 2)
 SLICE = 256
 LOW = -1e30
-BLOCKS = (2, 1, 3, 0)
+BLOCKS = (((2, 0, 4),), ((1, 0, 2), (3, 0, 2)), ((1, 2, 2), (3, 2, 2)), ((0, 0, 4),))
 
 
 def similar(rows, columns):
@@ -170,17 +170,19 @@
     half = 2 * SIDE * q_rows
     for k in range(SIDE):
         move(f"p{k}", pooled.at[k, pl.ds(half, half)], from_sib.at[k], "p", f"p{k}", sibling)
-    for d in STEPS:
-        move(f"pa{d}", send_a.at[d - 1], recv_a.at[back(d) - 1], "pa", "pa", along_y[d])
-        move(f"pb{d}", send_b.at[d - 1], recv_b.at[back(d) - 1], "pb", "pb", along_x[d])
-    ends = []
+    for runs in BLOCKS[:-1]:
+        for d, place, count in runs:
+            run = pl.ds(place, count)
+            move(f"pa{d}{place}", send_a.at[d - 1, run], recv_a.at[back(d) - 1, run], "pa", "pa", along_y[d])
+            move(f"pb{d}{place}", send_b.at[d - 1, run], recv_b.at[back(d) - 1, run], "pb", "pb", along_x[d])
+    ends = ([], [])
     for d in range(SIDE):
         for flip in (0, 1):
             for j, target in enumerate((device(dx=d, flip_lo=flip), device(dy=d, flip_hi=1, flip_lo=flip))):
                 if d or flip or j:
                     place = (flip * 2 + j) * SIDE
                     move(f"f{place + d}", windows.at[place + d], final.at[place + back(d)], "f", "f", target)
-                    ends.append(f"f{place + d}")
+                    ends[j].append(f"f{place + d}")
 
     bank_all[pl.ds(0, shard), :] = bank[...]
     peak[...] = jnp.full_like(peak, -jnp.inf)
@@ -209,36 +211,34 @@
         arrived("a12", unit("a20"))
         start("zb")
         arrived("c1", pair("a01"))
-        start("s1", "qz")
+        start("s1")
         from_other(0)
 
     def before_2():
         arrived("b12", unit("b02"))
         start("za")
         arrived("c2", pair("b10"))
-        start("s2", "qa11", "qa13", "qa12", "a221", "a223", "b221", "b223")
+        start("s2", "a221", "a223", "b221", "b223")
         from_other(1)
 
     def before_3():
         from_own(3)
-        arrived("qz", gather_b.at[0])
-        start("qb11", "qb13", "qb12")
         from_other(2)
 
     def before_4():
         from_own(4)
         start("ta", "tb", "a222", "b222")
-        from_other(3)
-
-    def before_5():
-        from_own(5)
         arrived("qa1", gather_a.at[pl.ds(1, SIDE - 1)])
         arrived("qb1", gather_b.at[pl.ds(1, SIDE - 1)])
         start("qa22", "qb22", "qas0", "qbs0")
+        from_other(3)
+
+    def before_5():
+        from_own(5)
+        start("qa21", "qa23", "qb21", "qb23")
         from_other(4)
 
     def before_6():
-        start("qa21", "qa23", "qb21", "qb23")
         from_own(6)
         from_other(5)
 
@@ -263,12 +263,13 @@
             scores[piece % 2, :count] = similar(bank_all[rows, :], refs[piece * SLICE:(piece + 1) * SLICE, :])
             absorb((piece + 1) % 2, (piece - 1) % slices, count if piece else before)
 
-    start("z", "a11", "a13", "a201", "a203", "a12")
+    start("z", "a11", "a13", "a201", "a203", "qz", "qa11", "qa13")
     arrived("z", unit("b00"))
-    start("b11", "b13")
+    start("b11", "b13", "a12", "qa12")
     for d, place in ((1, 3), (3, 1)):
         arrived(f"a1{d}", unit(f"a{place}0"))
-    start("b201", "b203", "b12", "s0")
+    arrived("qz", gather_b.at[0])
+    start("b201", "b203", "qb11", "qb13", "b12", "qb12", "s0")
     load.wait()
     score(0, part)
 
@@ -294,13 +295,15 @@
     for kind, gather in gathers.items():
         arrived(f"q{kind}s0", gather.at[pl.ds(plane, SIDE)])
         arrived(f"q{kind}s3", gather.at[pl.ds(plane + SIDE, plane - SIDE)])
-    for k, line in enumerate(BLOCKS):
+    for k, runs in enumerate(BLOCKS):
         for j, gather in enumerate((gather_a, gather_b)):
             for side in range(2):
-                first = side * plane + line * SIDE
-                rows = join_rows(gather[first:first + SIDE].astype(jnp.float32))
-                first = (2 * side + j) * quarter
-                q_all[k, first:first + quarter, :] = rows.reshape(quarter, width).astype(jnp.bfloat16)
+                row = (2 * side + j) * quarter
+                for line, place, count in runs:
+                    first = side * plane + line * SIDE + place
+                    rows = join_rows(gather[first:first + count].astype(jnp.float32)).astype(jnp.bfloat16)
+                    q_all[k, row:row + count * q_rows, :] = rows.reshape(count * q_rows, width)
+                    row += count * q_rows
 
     def pool(k, carry):
         block = q_all[k]
@@ -309,6 +312,7 @@
             tile = similar(block, refs[columns, :]).reshape(2 * half // 8, 8, SLICE)
             tile = 1.0 / (1.0 + jnp.exp(offset[:, columns][None] - tile))
             weights[:, columns] = tile.reshape(2 * half, SLICE).astype(jnp.bfloat16)
+        pl.when(k == SIDE - 1)(lambda: reduce_block(SIDE - 2))
         pooled[k] = jnp.dot(weights[...], refs[...], preferred_element_type=jnp.float32)
         for j in range(SIDE):
             pl.when(k == j)(lambda j=j: after_pool(j))
@@ -316,7 +320,7 @@
 
     def after_pool(k):
         start(f"p{k}")
-        if k >= 1:
+        if 1 <= k < SIDE - 1:
             reduce_block(k - 1)
 
     def both_cores(k):
@@ -325,10 +329,12 @@
         return [rows[j * quarter:(j + 1) * quarter].reshape(SIDE, q_rows, width) for j in range(2)]
 
     def reduce_block(k):
-        line = BLOCKS[k]
-        for rows, send in zip(both_cores(k), (send_a, send_b)):
-            send[line - 1] = split_rows(rows).astype(jnp.bfloat16)
-        start(f"pa{line}", f"pb{line}")
+        for kind, rows, send in zip("ab", both_cores(k), (send_a, send_b)):
+            first = 0
+            for line, place, count in BLOCKS[k]:
+                send[line - 1, place:place + count] = split_rows(rows[first:first + count]).astype(jnp.bfloat16)
+                start(f"p{kind}{line}{place}")
+                first += count
 
     lax.fori_loop(0, SIDE, pool, 0)
     same_lo = pl.ds(pl.multiple_of(8 * z_lo, 8), WINDOW)
@@ -339,7 +345,7 @@
         for flip, lo in enumerate((same_lo, other_lo)):
             first = (flip * 2 + j) * SIDE
             windows[first:first + SIDE] = sums[j, :, lo, :].astype(jnp.bfloat16)
-    start(*ends)
+        start(*ends[j])
     rows = sums[0, 0, same_lo, :]
     own = queries[...].astype(jnp.float32)
     own = jnp.where(z_lo == 0, own[:WINDOW], own[q_rows - WINDOW:])

time: 57.9 us -> 56.7 us (0.979)
  Pallas kernels: 56.3 us -> 55 us
    pallas_call x1, Pallas kernels: 56.3 us -> 55 us  [per_device(): pl.pallas_call(kernel, out_shape=jax.ShapeDtypeStruct((q_rows // 2, width...]
where the time goes in v4:
time: 56.7 us; the launch traced here: 56.4 us
  Pallas kernels  55 us (97%)
  local copies, waits for them, and re-layouts  1.38 us (2%)
    pallas_call x1, Pallas kernels, per_device(): pl.pallas_call(kernel, out_shape=jax.ShapeDtypeStruct((q_rows // 2, width...  55 us
    unnamed x1, local copies, waits for them, and re-layouts  1.38 us

profile of v4, /device:TPU:1, one launch (start us, length us, event | category | flops | bytes accessed | tf_op | source)
XLA Modules:
  0.0 56.4 jit_solution(16935516216263627374)
XLA Ops:
  0.0 55.0 %shard_map.37 = f32[12,512]{1,0:T(8,128)} custom-call(bf16[2048,512]{1,0:T(8,128)(2,1)} %refs_hbm.1, bf16[96,512]{1,0:T(8,128)(2,1)} %bank.1, bf16[24,512]{1,0:T(8,128)(2,1)} %queries.1), custom_call_target="tpu_custom_call" | custom-call | tf_op jit(solution)/shard_map/pallas_call | solution.py:378
  55.1 1.4 %copy.5 = f32[12,512]{1,0:T(8,128)} copy(f32[12,512]{1,0:T(8,128)} %shard_map.37) | data formatting | bytes 49152

commit v5 on v4

--- a/solution.py
+++ b/solution.py
@@ -207,7 +207,7 @@
     def before_1():
         for d, place in ((1, 3), (3, 1)):
             arrived(f"b1{d}", unit(f"b0{place}"))
-        start("a211", "a213", "b211", "b213", "a2n", "b2n", "a231", "a233", "b231", "b233")
+        start("a211", "a213", "b211", "b213", "a2n", "b2n")
         arrived("a12", unit("a20"))
         start("zb")
         arrived("c1", pair("a01"))
@@ -216,7 +216,7 @@
 
     def before_2():
         arrived("b12", unit("b02"))
-        start("za")
+        start("za", "a231", "a233", "b231", "b233")
         arrived("c2", pair("b10"))
         start("s2", "a221", "a223", "b221", "b223")
         from_other(1)
@@ -305,18 +305,17 @@
                     q_all[k, row:row + count * q_rows, :] = rows.reshape(count * q_rows, width)
                     row += count * q_rows
 
-    def pool(k, carry):
+    def pool(k):
         block = q_all[k]
         for piece in range(slices):
             columns = slice(piece * SLICE, (piece + 1) * SLICE)
             tile = similar(block, refs[columns, :]).reshape(2 * half // 8, 8, SLICE)
             tile = 1.0 / (1.0 + jnp.exp(offset[:, columns][None] - tile))
             weights[:, columns] = tile.reshape(2 * half, SLICE).astype(jnp.bfloat16)
-        pl.when(k == SIDE - 1)(lambda: reduce_block(SIDE - 2))
+        if k == SIDE - 1:
+            reduce_block(SIDE - 2)
         pooled[k] = jnp.dot(weights[...], refs[...], preferred_element_type=jnp.float32)
-        for j in range(SIDE):
-            pl.when(k == j)(lambda j=j: after_pool(j))
-        return carry
+        after_pool(k)
 
     def after_pool(k):
         start(f"p{k}")
@@ -336,7 +335,8 @@
                 start(f"p{kind}{line}{place}")
                 first += count
 
-    lax.fori_loop(0, SIDE, pool, 0)
+    for k in range(SIDE):
+        pool(k)
     same_lo = pl.ds(pl.multiple_of(8 * z_lo, 8), WINDOW)
     other_lo = pl.ds(pl.multiple_of(8 * (1 - z_lo), 8), WINDOW)
     for j, (rows, recv) in enumerate(zip(both_cores(SIDE - 1), (recv_a, recv_b))):

time: 56.7 us -> 55.5 us (0.979)
  Pallas kernels: 55 us -> 53.9 us
    pallas_call x1, Pallas kernels: 55 us -> 53.9 us  [per_device(): pl.pallas_call(kernel, out_shape=jax.ShapeDtypeStruct((q_rows // 2, width...]
where the time goes in v5:
time: 55.5 us; the launch traced here: 55.3 us
  Pallas kernels  53.9 us (97%)
  local copies, waits for them, and re-layouts  1.38 us (2%)
    pallas_call x1, Pallas kernels, per_device(): pl.pallas_call(kernel, out_shape=jax.ShapeDtypeStruct((q_rows // 2, width...  53.9 us
    unnamed x1, local copies, waits for them, and re-layouts  1.38 us

profile of v5, /device:TPU:1, one launch (start us, length us, event | category | flops | bytes accessed | tf_op | source)
XLA Modules:
  0.0 55.3 jit_solution(9591049659258113482)
XLA Ops:
  0.0 53.9 %shard_map.37 = f32[12,512]{1,0:T(8,128)} custom-call(bf16[2048,512]{1,0:T(8,128)(2,1)} %refs_hbm.1, bf16[96,512]{1,0:T(8,128)(2,1)} %bank.1, bf16[24,512]{1,0:T(8,128)(2,1)} %queries.1), custom_call_target="tpu_custom_call" | custom-call | tf_op jit(solution)/shard_map/pallas_call | solution.py:378
  53.9 1.4 %copy.5 = f32[12,512]{1,0:T(8,128)} copy(f32[12,512]{1,0:T(8,128)} %shard_map.37) | data formatting | bytes 49152

commit v6 on v5

--- a/solution.py
+++ b/solution.py
@@ -184,17 +184,17 @@
                     move(f"f{place + d}", windows.at[place + d], final.at[place + back(d)], "f", "f", target)
                     ends[j].append(f"f{place + d}")
 
+    partners = [sibling, twin, facing, device(flip_hi=1), *along_x.values(), *along_y.values()]
+    barrier = pltpu.get_barrier_semaphore()
+    for partner in partners:
+        pl.semaphore_signal(barrier, inc=1, device_id=partner, device_id_type=MESH)
+
     bank_all[pl.ds(0, shard), :] = bank[...]
     peak[...] = jnp.full_like(peak, -jnp.inf)
     total[...] = jnp.zeros_like(total)
     scores[1] = jnp.full(scores.shape[1:], LOW, jnp.float32)
     own_q[...] = split_rows(queries[...].astype(jnp.float32)[None])[0].astype(jnp.bfloat16)
     gather_a[0] = own_q[...]
-
-    partners = [sibling, twin, facing, device(flip_hi=1), *along_x.values(), *along_y.values()]
-    barrier = pltpu.get_barrier_semaphore()
-    for partner in partners:
-        pl.semaphore_signal(barrier, inc=1, device_id=partner, device_id_type=MESH)
     pl.semaphore_wait(barrier, len(partners))
 
     def from_own(k):

time: 55.5 us -> 55.4 us (level)
  no operation moved by 1% of the time
where the time goes in v6:
time: 55.4 us; the launch traced here: 55.1 us
  Pallas kernels  53.8 us (97%)
  local copies, waits for them, and re-layouts  1.38 us (2%)
    pallas_call x1, Pallas kernels, per_device(): pl.pallas_call(kernel, out_shape=jax.ShapeDtypeStruct((q_rows // 2, width...  53.8 us
    unnamed x1, local copies, waits for them, and re-layouts  1.38 us

profile of v6, /device:TPU:1, one launch (start us, length us, event | category | flops | bytes accessed | tf_op | source)
XLA Modules:
  0.0 55.1 jit_solution(4206688180287060719)
XLA Ops:
  0.0 53.8 %shard_map.37 = f32[12,512]{1,0:T(8,128)} custom-call(bf16[2048,512]{1,0:T(8,128)(2,1)} %refs_hbm.1, bf16[96,512]{1,0:T(8,128)(2,1)} %bank.1, bf16[24,512]{1,0:T(8,128)(2,1)} %queries.1), custom_call_target="tpu_custom_call" | custom-call | tf_op jit(solution)/shard_map/pallas_call | solution.py:378
  53.8 1.4 %copy.5 = f32[12,512]{1,0:T(8,128)} copy(f32[12,512]{1,0:T(8,128)} %shard_map.37) | data formatting | bytes 49152
